TPU v7x, 32 devices: a whole 2x2x4 slice. The times are simulated.
32 devices in a mesh: grp: 4 (over x, core), tile: 8 (over z, y).
Axes of the slice: x: 2, y: 2, z: 4, core: 2. Of those that a mesh axis runs over, the one named last changes fastest.
Arguments:
- height_model: float32 [4608, 1024], P('grp', 'tile'), as said below
- scenario_trigger_indicator: int32 [4, 256, 512], P('grp', 'tile'), may hold values 0 or 1
- initial_snow_thickness_cm: int32 [4, 256, 512], P('grp', 'tile'), may hold values from 20 to 300
- frame_leading_northing_index: int32 [4], P('grp'), may hold values from 3 to 4349
- frame_leading_easting_index: int32 [4], P('grp'), may hold values from 3 to 509
Outputs:
- ground_geometry: float32 [4, 4608, 1024], P(None, 'grp', 'tile')
- flow: float32 [4, 3, 256, 512], P('grp', None, 'tile')
Inputs may be any that keep to these rules, and one draw needn't show every extreme that they name: `frame_leading_northing_index`: each window, widened by 3 cells on every side, lies inside the DEM rows. `frame_leading_easting_index`: each window, widened by 3 cells on every side, lies inside the DEM columns. `height_model`: elevation in metres, near zero at the DEM's rim within a few metres.
All inputs are finite; a program needn't handle non-finite values. No bound on the sum of `scenario_trigger_indicator` on one device may be relied on, other than what follows from the above.
Results may differ from a plain program's by a relative error of at most 0.0003.
Values sent between devices are 32-bit elements; how exact they have to be, the bound alone decides.
A program may use at most 64 MiB of HBM per device.

v0:
```python
import jax
import jax.numpy as jnp
from jax import lax
from jax.sharding import PartitionSpec as P

KERNEL_SPAN = 3
STEPS = 4


cell_size = 2.0
gravity = 9.81
time_step = 0.1
friction = 0.2
turbulence = 500.0
depth_floor = 0.1
speed_floor = 0.5
binomial = (0.0625, 0.25, 0.375, 0.25, 0.0625)


def padded(shard, sides, width):
    for axis, dim in sides:
        size, length = (lax.axis_size(axis), shard.shape[dim])
        up = [(i, (i + 1) % size) for i in range(size - 1)]
        down = [(j, i) for i, j in up]
        last = lax.slice_in_dim(shard, length - width, length, axis=dim)
        leading = lax.slice_in_dim(shard, 0, width, axis=dim)
        before = lax.ppermute(last, axis, up)
        after = lax.ppermute(leading, axis, down)
        shard = jnp.concatenate([before, shard, after], axis=dim)
    return shard


def derive_gradient_fields(framed_elevation_grid):
    inner_rows = framed_elevation_grid.shape[0] - 2 * KERNEL_SPAN
    inner_cols = framed_elevation_grid.shape[1] - 2 * KERNEL_SPAN
    across = binomial[0] * framed_elevation_grid[0 : inner_rows + 2, :]
    for offset in range(1, 5):
        across = (
            across + binomial[offset] * framed_elevation_grid[offset : offset + inner_rows + 2, :]
        )
    smooth = binomial[0] * across[:, 0 : inner_cols + 2]
    for offset in range(1, 5):
        smooth = smooth + binomial[offset] * across[:, offset : offset + inner_cols + 2]
    centre = smooth[1:-1, 1:-1]
    upper_cell = smooth[2:, 1:-1]
    lower_cell = smooth[:-2, 1:-1]
    right_cell = smooth[1:-1, 2:]
    left_cell = smooth[1:-1, :-2]
    grad_rows = (upper_cell - lower_cell) / (2.0 * cell_size)
    grad_cols = (right_cell - left_cell) / (2.0 * cell_size)
    curvature = (upper_cell + lower_cell + right_cell + left_cell - 4.0 * centre) / (
        cell_size * cell_size
    )
    upright = 1.0 / jnp.sqrt(1.0 + grad_rows * grad_rows + grad_cols * grad_cols)
    return jnp.stack([-grad_rows * upright, -grad_cols * upright, upright, curvature])


def advance(framed_elevation_grid, patch):
    depth_now = framed_elevation_grid[0]
    momentum_a = framed_elevation_grid[1]
    momentum_b = framed_elevation_grid[2]
    safe_depth = jnp.maximum(depth_now, depth_floor)
    velocity_a = momentum_a / safe_depth
    velocity_b = momentum_b / safe_depth
    wave_speed = jnp.sqrt(gravity * (jnp.maximum(depth_now, 0.0) + depth_floor))
    pressure = 0.5 * gravity * depth_now * depth_now
    flux_rows = jnp.stack([momentum_a, momentum_a * velocity_a + pressure, momentum_b * velocity_a])
    flux_cols = jnp.stack([momentum_b, momentum_a * velocity_b, momentum_b * velocity_b + pressure])
    reach_rows = jnp.abs(velocity_a) + wave_speed
    reach_cols = jnp.abs(velocity_b) + wave_speed
    bound_rows = jnp.maximum(reach_rows[:-1, 1:-1], reach_rows[1:, 1:-1])
    face_rows = 0.5 * (flux_rows[:, :-1, 1:-1] + flux_rows[:, 1:, 1:-1]) - 0.5 * bound_rows * (
        framed_elevation_grid[:, 1:, 1:-1] - framed_elevation_grid[:, :-1, 1:-1]
    )
    bound_cols = jnp.maximum(reach_cols[1:-1, :-1], reach_cols[1:-1, 1:])
    face_cols = 0.5 * (flux_cols[:, 1:-1, :-1] + flux_cols[:, 1:-1, 1:]) - 0.5 * bound_cols * (
        framed_elevation_grid[:, 1:-1, 1:] - framed_elevation_grid[:, 1:-1, :-1]
    )
    interior = framed_elevation_grid[:, 1:-1, 1:-1]
    updated = interior - time_step / cell_size * (
        face_rows[:, 1:] - face_rows[:, :-1] + face_cols[:, :, 1:] - face_cols[:, :, :-1]
    )
    new_depth = updated[0]
    drive_a = updated[1] + time_step * gravity * interior[0] * patch[0]
    drive_b = updated[2] + time_step * gravity * interior[0] * patch[1]
    floor_depth = jnp.maximum(new_depth, depth_floor)
    rate_a = drive_a / floor_depth
    rate_b = drive_b / floor_depth
    square = rate_a * rate_a + rate_b * rate_b
    speed_norm = jnp.sqrt(square + speed_floor * speed_floor)
    normal_load = jnp.maximum(gravity * patch[2] + patch[3] * square, 0.0)
    drag_factor = time_step * (
        friction * normal_load / speed_norm + gravity * speed_norm / (turbulence * floor_depth)
    )
    return jnp.stack([new_depth, drive_a / (1.0 + drag_factor), drive_b / (1.0 + drag_factor)])


def shards(
    height_model,
    scenario_trigger_indicator,
    initial_snow_thickness_cm,
    frame_leading_northing_index,
    frame_leading_easting_index,
):
    tile_count = lax.axis_size("tile")
    piece_rows = scenario_trigger_indicator.shape[1]
    window_width = scenario_trigger_indicator.shape[2]
    window_height = piece_rows * tile_count
    block_lateral_number = height_model.shape[1]
    framed_elevation_grid = padded(height_model, (("grp", 0), ("tile", 1)), KERNEL_SPAN)
    ground_geometry = derive_gradient_fields(framed_elevation_grid)
    first_row = frame_leading_northing_index[0]
    first_col = frame_leading_easting_index[0]
    column_strip = lax.all_gather(ground_geometry, "grp", axis=1, tiled=True)
    row_band = lax.dynamic_slice_in_dim(column_strip, first_row, window_height, 1)
    blocks = row_band.reshape(4, tile_count, piece_rows, block_lateral_number)
    rows_wide = lax.all_to_all(blocks, "tile", split_axis=1, concat_axis=3, tiled=True)
    rows_wide = rows_wide.reshape(4, piece_rows, tile_count * block_lateral_number)
    under_window = lax.dynamic_slice_in_dim(rows_wide, first_col, window_width, 2)
    release_depth = (
        scenario_trigger_indicator[0].astype(jnp.float32)
        * initial_snow_thickness_cm[0].astype(jnp.float32)
        * 0.01
    )
    empty_field = jnp.zeros_like(release_depth)
    flow_state = jnp.stack([release_depth, empty_field, empty_field])
    for turn_index in range(STEPS):
        extended = padded(flow_state, (("tile", 1),), 1)
        flow_state = advance(jnp.pad(extended, ((0, 0), (0, 0), (1, 1))), under_window)
    return (ground_geometry, flow_state[None])


def solution(mesh):
    return jax.shard_map(
        shards,
        mesh=mesh,
        in_specs=(
            P("grp", "tile"),
            P("grp", "tile", None),
            P("grp", "tile", None),
            P("grp"),
            P("grp"),
        ),
        out_specs=(P(None, "grp", "tile"), P("grp", None, "tile", None)),
        check_vma=False,
    )
```

profile of v0, /device:TPU:16, one launch (start us, length us, event | category | flops | bytes accessed | tf_op | source)
XLA Modules:
  0.0 159.4 jit_solution(9979088048718649279)
XLA Ops:
  7.9 1.7 %collective-permute-start = (f32[3,128]{1,0:T(4,128)S(1)}, f32[3,128]{1,0:T(4,128)S(1)}, u32[]{:S(2)}, u32[]{:S(2)}) collective-permute-start(f32[3,128]{1,0:T(4,128)S(1)} %get-tuple-element.21), channel_id=1, source_target_pairs={{0,8},{8,16},{16,24},{1,9},{9,17},{17,25},{2,10},{10,18},{18,26},{... | collective-permute-start | bytes 4616 | tf_op jit(solution)/shard_map/ppermute | solution.py:27
  9.7 1.3 collective-permute-start.1
  11.0 3.0 %collective-permute-done.1 = f32[3,128]{1,0:T(4,128)S(1)} collective-permute-done((f32[3,128]{1,0:T(4,128)S(1)}, f32[3,128]{1,0:T(4,128)S(1)}, u32[]{:S(2)}, u32[]{:S(2)}) %collective-permute-start.1) | collective-permute-done | bytes 1568 | tf_op jit(solution)/shard_map/ppermute | solution.py:28
  14.0 2.3 %concatenate.42 = f32[1158,128]{1,0:T(8,128)S(1)} concatenate(f32[3,128]{1,0:T(4,128)S(1)} %collective-permute-done, f32[1152,128]{1,0:T(8,128)} %param.5, f32[3,128]{1,0:T(4,128)S(1)} %collective-permute-done.1), dimensions={0} | concatenate | bytes 1185792 | tf_op jit(solution)/shard_map/concatenate | solution.py:29
  16.7 3.3 %collective-permute-start.3 = (f32[1158,3]{0,1:T(4,128)S(1)}, f32[1158,3]{0,1:T(4,128)S(1)}, u32[]{:S(2)}, u32[]{:S(2)}) collective-permute-start(f32[1158,3]{0,1:T(4,128)S(1)} %copy.9), channel_id=1, source_target_pairs={{1,0},{2,1},{3,2},{4,3},{5,4},{6,5},{7,6},{9,8},{10,9},{11,10},{12... | collective-permute-start | bytes 41696 | tf_op jit(solution)/shard_map/ppermute | solution.py:28
  20.2 2.5 %collective-permute-start.2 = (f32[1158,3]{0,1:T(4,128)S(1)}, f32[1158,3]{0,1:T(4,128)S(1)}, u32[]{:S(2)}, u32[]{:S(2)}) collective-permute-start(f32[1158,3]{0,1:T(4,128)S(1)} %copy.8), channel_id=1, source_target_pairs={{0,1},{1,2},{2,3},{3,4},{4,5},{5,6},{6,7},{8,9},{9,10},{10,11},{11... | collective-permute-start | bytes 41696 | tf_op jit(solution)/shard_map/ppermute | solution.py:27
  23.1 3.8 %collective-permute-done.2 = f32[1158,3]{0,1:T(4,128)S(1)} collective-permute-done((f32[1158,3]{0,1:T(4,128)S(1)}, f32[1158,3]{0,1:T(4,128)S(1)}, u32[]{:S(2)}, u32[]{:S(2)}) %collective-permute-start.2) | collective-permute-done | bytes 13928 | tf_op jit(solution)/shard_map/ppermute | solution.py:27
  28.3 1.3 fusion
  30.3 1.6 pad_maximum_fusion
  32.8 1.9 %collective-permute-start.5 = (f32[3,1,512]{2,1,0:T(1,128)S(1)}, f32[3,1,512]{2,1,0:T(1,128)S(1)}, u32[]{:S(2)}, u32[]{:S(2)}) collective-permute-start(f32[3,1,512]{2,1,0:T(1,128)S(1)} %get-tuple-element.65), channel_id=1, source_target_pairs={{1,0},{2,1},{3,2},{4,3},{5,4},{6,5},{7,6},{9,8},{10,9},{11,10},{12... | collective-permute-start | bytes 18440 | tf_op jit(solution)/shard_map/ppermute | solution.py:28
  34.7 3.9 %collective-permute-start.4 = (f32[3,1,512]{2,1,0:T(1,128)S(1)}, f32[3,1,512]{2,1,0:T(1,128)S(1)}, u32[]{:S(2)}, u32[]{:S(2)}) collective-permute-start(f32[3,1,512]{2,1,0:T(1,128)S(1)} %get-tuple-element.64), channel_id=1, source_target_pairs={{0,1},{1,2},{2,3},{3,4},{4,5},{5,6},{6,7},{8,9},{9,10},{10,11},{11... | collective-permute-start | bytes 18440 | tf_op jit(solution)/shard_map/ppermute | solution.py:27
  40.0 1.1 collective-permute-done.4
  41.6 55.6 %all-gather.2.cloned.1.call-done = f32[4,4608,128]{2,1,0:T(8,128)} async-done(((f32[4,1152,128]{2,1,0:T(8,128)}), f32[4,4608,128]{2,1,0:T(8,128)}) %all-gather.2.cloned.1.call-update) | async-done | bytes 9437200 | tf_op jit(solution)/shard_map/all_gather | solution.py:114
  99.1 6.0 %all-to-all-start = ((f32[4,8,32,128]{3,2,0,1:T(8,128)}), f32[4,8,32,128]{3,2,0,1:T(8,128)S(1)}, u32[]{:S(2)}, u32[]{:S(2)}) async-start(f32[4,8,32,128]{3,2,0,1:T(8,128)} %copy.12), calls=%async_computation | async-start | bytes 1048576 | tf_op jit(solution)/shard_map/all_to_all | solution.py:117
  105.8 11.5 %all-to-all-done = f32[4,8,32,128]{3,2,0,1:T(8,128)S(1)} async-done(((f32[4,8,32,128]{3,2,0,1:T(8,128)}), f32[4,8,32,128]{3,2,0,1:T(8,128)S(1)}, u32[]{:S(2)}, u32[]{:S(2)}) %all-to-all-start) | async-done | bytes 524320 | tf_op jit(solution)/shard_map/all_to_all | solution.py:117
  117.9 2.9 %collective-permute-start.7 = (f32[3,1,512]{2,1,0:T(1,128)S(1)}, f32[3,1,512]{2,1,0:T(1,128)S(1)}, u32[]{:S(2)}, u32[]{:S(2)}) collective-permute-start(f32[3,1,512]{2,1,0:T(1,128)S(1)} %get-tuple-element.62), channel_id=1, source_target_pairs={{1,0},{2,1},{3,2},{4,3},{5,4},{6,5},{7,6},{9,8},{10,9},{11,10},{12... | collective-permute-start | bytes 18440 | tf_op jit(solution)/shard_map/ppermute | solution.py:28
  120.8 3.0 %collective-permute-start.6 = (f32[3,1,512]{2,1,0:T(1,128)S(1)}, f32[3,1,512]{2,1,0:T(1,128)S(1)}, u32[]{:S(2)}, u32[]{:S(2)}) collective-permute-start(f32[3,1,512]{2,1,0:T(1,128)S(1)} %get-tuple-element.61), channel_id=1, source_target_pairs={{0,1},{1,2},{2,3},{3,4},{4,5},{5,6},{6,7},{8,9},{9,10},{10,11},{11... | collective-permute-start | bytes 18440 | tf_op jit(solution)/shard_map/ppermute | solution.py:27
  123.8 3.4 %collective-permute-done.6 = f32[3,1,512]{2,1,0:T(1,128)S(1)} collective-permute-done((f32[3,1,512]{2,1,0:T(1,128)S(1)}, f32[3,1,512]{2,1,0:T(1,128)S(1)}, u32[]{:S(2)}, u32[]{:S(2)}) %collective-permute-start.6) | collective-permute-done | bytes 6176 | tf_op jit(solution)/shard_map/ppermute | solution.py:27
  128.6 3.7 %collective-permute-start.9 = (f32[3,1,512]{2,1,0:T(1,128)S(1)}, f32[3,1,512]{2,1,0:T(1,128)S(1)}, u32[]{:S(2)}, u32[]{:S(2)}) collective-permute-start(f32[3,1,512]{2,1,0:T(1,128)S(1)} %get-tuple-element.59), channel_id=1, source_target_pairs={{1,0},{2,1},{3,2},{4,3},{5,4},{6,5},{7,6},{9,8},{10,9},{11,10},{12... | collective-permute-start | bytes 18440 | tf_op jit(solution)/shard_map/ppermute | solution.py:28
  132.3 2.1 %collective-permute-start.8 = (f32[3,1,512]{2,1,0:T(1,128)S(1)}, f32[3,1,512]{2,1,0:T(1,128)S(1)}, u32[]{:S(2)}, u32[]{:S(2)}) collective-permute-start(f32[3,1,512]{2,1,0:T(1,128)S(1)} %get-tuple-element.58), channel_id=1, source_target_pairs={{0,1},{1,2},{2,3},{3,4},{4,5},{5,6},{6,7},{8,9},{9,10},{10,11},{11... | collective-permute-start | bytes 18440 | tf_op jit(solution)/shard_map/ppermute | solution.py:27
  134.5 4.3 %collective-permute-done.8 = f32[3,1,512]{2,1,0:T(1,128)S(1)} collective-permute-done((f32[3,1,512]{2,1,0:T(1,128)S(1)}, f32[3,1,512]{2,1,0:T(1,128)S(1)}, u32[]{:S(2)}, u32[]{:S(2)}) %collective-permute-start.8) | collective-permute-done | bytes 6176 | tf_op jit(solution)/shard_map/ppermute | solution.py:27
  140.1 3.9 %collective-permute-start.11 = (f32[3,1,512]{2,1,0:T(1,128)S(1)}, f32[3,1,512]{2,1,0:T(1,128)S(1)}, u32[]{:S(2)}, u32[]{:S(2)}) collective-permute-start(f32[3,1,512]{2,1,0:T(1,128)S(1)} %get-tuple-element.56), channel_id=1, source_target_pairs={{1,0},{2,1},{3,2},{4,3},{5,4},{6,5},{7,6},{9,8},{10,9},{11,10},{12... | collective-permute-start | bytes 18440 | tf_op jit(solution)/shard_map/ppermute | solution.py:28
  144.1 1.9 %collective-permute-start.10 = (f32[3,1,512]{2,1,0:T(1,128)S(1)}, f32[3,1,512]{2,1,0:T(1,128)S(1)}, u32[]{:S(2)}, u32[]{:S(2)}) collective-permute-start(f32[3,1,512]{2,1,0:T(1,128)S(1)} %get-tuple-element.55), channel_id=1, source_target_pairs={{0,1},{1,2},{2,3},{3,4},{4,5},{5,6},{6,7},{8,9},{9,10},{10,11},{11... | collective-permute-start | bytes 18440 | tf_op jit(solution)/shard_map/ppermute | solution.py:27
  146.0 4.5 %collective-permute-done.10 = f32[3,1,512]{2,1,0:T(1,128)S(1)} collective-permute-done((f32[3,1,512]{2,1,0:T(1,128)S(1)}, f32[3,1,512]{2,1,0:T(1,128)S(1)}, u32[]{:S(2)}, u32[]{:S(2)}) %collective-permute-start.10) | collective-permute-done | bytes 6176 | tf_op jit(solution)/shard_map/ppermute | solution.py:27
  (78 shorter events, 12.9 us)
Async XLA Ops:
  7.2 90.0 %all-gather.2.cloned.1.call-start = ((), (), s32[]{:S(2)}) async-start(), calls=%async_computation.1 | async-start | bytes 11796480 | tf_op jit(solution)/shard_map/all_gather | solution.py:114
  7.9 3.0 %collective-permute-start = (f32[3,128]{1,0:T(4,128)S(1)}, f32[3,128]{1,0:T(4,128)S(1)}, u32[]{:S(2)}, u32[]{:S(2)}) collective-permute-start(f32[3,128]{1,0:T(4,128)S(1)} %get-tuple-element.21), channel_id=1, source_target_pairs={{0,8},{8,16},{16,24},{1,9},{9,17},{17,25},{2,10},{10,18},{18,26},{... | collective-permute-start | bytes 4616 | tf_op jit(solution)/shard_map/ppermute | solution.py:27
  9.7 4.3 %collective-permute-start.1 = (f32[3,128]{1,0:T(4,128)S(1)}, f32[3,128]{1,0:T(4,128)S(1)}, u32[]{:S(2)}, u32[]{:S(2)}) collective-permute-start(f32[3,128]{1,0:T(4,128)S(1)} %get-tuple-element.20), channel_id=1, source_target_pairs={{8,0},{16,8},{24,16},{9,1},{17,9},{25,17},{10,2},{18,10},{26,18},{... | collective-permute-start | bytes 4616 | tf_op jit(solution)/shard_map/ppermute | solution.py:28
  16.7 6.1 %collective-permute-start.3 = (f32[1158,3]{0,1:T(4,128)S(1)}, f32[1158,3]{0,1:T(4,128)S(1)}, u32[]{:S(2)}, u32[]{:S(2)}) collective-permute-start(f32[1158,3]{0,1:T(4,128)S(1)} %copy.9), channel_id=1, source_target_pairs={{1,0},{2,1},{3,2},{4,3},{5,4},{6,5},{7,6},{9,8},{10,9},{11,10},{12... | collective-permute-start | bytes 41696 | tf_op jit(solution)/shard_map/ppermute | solution.py:28
  20.2 6.6 %collective-permute-start.2 = (f32[1158,3]{0,1:T(4,128)S(1)}, f32[1158,3]{0,1:T(4,128)S(1)}, u32[]{:S(2)}, u32[]{:S(2)}) collective-permute-start(f32[1158,3]{0,1:T(4,128)S(1)} %copy.8), channel_id=1, source_target_pairs={{0,1},{1,2},{2,3},{3,4},{4,5},{5,6},{6,7},{8,9},{9,10},{10,11},{11... | collective-permute-start | bytes 41696 | tf_op jit(solution)/shard_map/ppermute | solution.py:27
  31.9 0.8 copy-start
  31.9 0.9 copy-start.1
  32.8 7.2 %collective-permute-start.5 = (f32[3,1,512]{2,1,0:T(1,128)S(1)}, f32[3,1,512]{2,1,0:T(1,128)S(1)}, u32[]{:S(2)}, u32[]{:S(2)}) collective-permute-start(f32[3,1,512]{2,1,0:T(1,128)S(1)} %get-tuple-element.65), channel_id=1, source_target_pairs={{1,0},{2,1},{3,2},{4,3},{5,4},{6,5},{7,6},{9,8},{10,9},{11,10},{12... | collective-permute-start | bytes 18440 | tf_op jit(solution)/shard_map/ppermute | solution.py:28
  34.7 6.4 %collective-permute-start.4 = (f32[3,1,512]{2,1,0:T(1,128)S(1)}, f32[3,1,512]{2,1,0:T(1,128)S(1)}, u32[]{:S(2)}, u32[]{:S(2)}) collective-permute-start(f32[3,1,512]{2,1,0:T(1,128)S(1)} %get-tuple-element.64), channel_id=1, source_target_pairs={{0,1},{1,2},{2,3},{3,4},{4,5},{5,6},{6,7},{8,9},{9,10},{10,11},{11... | collective-permute-start | bytes 18440 | tf_op jit(solution)/shard_map/ppermute | solution.py:27
  99.1 18.2 %all-to-all-start = ((f32[4,8,32,128]{3,2,0,1:T(8,128)}), f32[4,8,32,128]{3,2,0,1:T(8,128)S(1)}, u32[]{:S(2)}, u32[]{:S(2)}) async-start(f32[4,8,32,128]{3,2,0,1:T(8,128)} %copy.12), calls=%async_computation | async-start | bytes 1048576 | tf_op jit(solution)/shard_map/all_to_all | solution.py:117
  117.9 5.9 %collective-permute-start.7 = (f32[3,1,512]{2,1,0:T(1,128)S(1)}, f32[3,1,512]{2,1,0:T(1,128)S(1)}, u32[]{:S(2)}, u32[]{:S(2)}) collective-permute-start(f32[3,1,512]{2,1,0:T(1,128)S(1)} %get-tuple-element.62), channel_id=1, source_target_pairs={{1,0},{2,1},{3,2},{4,3},{5,4},{6,5},{7,6},{9,8},{10,9},{11,10},{12... | collective-permute-start | bytes 18440 | tf_op jit(solution)/shard_map/ppermute | solution.py:28
  120.8 6.4 %collective-permute-start.6 = (f32[3,1,512]{2,1,0:T(1,128)S(1)}, f32[3,1,512]{2,1,0:T(1,128)S(1)}, u32[]{:S(2)}, u32[]{:S(2)}) collective-permute-start(f32[3,1,512]{2,1,0:T(1,128)S(1)} %get-tuple-element.61), channel_id=1, source_target_pairs={{0,1},{1,2},{2,3},{3,4},{4,5},{5,6},{6,7},{8,9},{9,10},{10,11},{11... | collective-permute-start | bytes 18440 | tf_op jit(solution)/shard_map/ppermute | solution.py:27
  128.6 5.9 %collective-permute-start.9 = (f32[3,1,512]{2,1,0:T(1,128)S(1)}, f32[3,1,512]{2,1,0:T(1,128)S(1)}, u32[]{:S(2)}, u32[]{:S(2)}) collective-permute-start(f32[3,1,512]{2,1,0:T(1,128)S(1)} %get-tuple-element.59), channel_id=1, source_target_pairs={{1,0},{2,1},{3,2},{4,3},{5,4},{6,5},{7,6},{9,8},{10,9},{11,10},{12... | collective-permute-start | bytes 18440 | tf_op jit(solution)/shard_map/ppermute | solution.py:28
  132.3 6.4 %collective-permute-start.8 = (f32[3,1,512]{2,1,0:T(1,128)S(1)}, f32[3,1,512]{2,1,0:T(1,128)S(1)}, u32[]{:S(2)}, u32[]{:S(2)}) collective-permute-start(f32[3,1,512]{2,1,0:T(1,128)S(1)} %get-tuple-element.58), channel_id=1, source_target_pairs={{0,1},{1,2},{2,3},{3,4},{4,5},{5,6},{6,7},{8,9},{9,10},{10,11},{11... | collective-permute-start | bytes 18440 | tf_op jit(solution)/shard_map/ppermute | solution.py:27
  140.1 5.9 %collective-permute-start.11 = (f32[3,1,512]{2,1,0:T(1,128)S(1)}, f32[3,1,512]{2,1,0:T(1,128)S(1)}, u32[]{:S(2)}, u32[]{:S(2)}) collective-permute-start(f32[3,1,512]{2,1,0:T(1,128)S(1)} %get-tuple-element.56), channel_id=1, source_target_pairs={{1,0},{2,1},{3,2},{4,3},{5,4},{6,5},{7,6},{9,8},{10,9},{11,10},{12... | collective-permute-start | bytes 18440 | tf_op jit(solution)/shard_map/ppermute | solution.py:28
  144.1 6.4 %collective-permute-start.10 = (f32[3,1,512]{2,1,0:T(1,128)S(1)}, f32[3,1,512]{2,1,0:T(1,128)S(1)}, u32[]{:S(2)}, u32[]{:S(2)}) collective-permute-start(f32[3,1,512]{2,1,0:T(1,128)S(1)} %get-tuple-element.55), channel_id=1, source_target_pairs={{0,1},{1,2},{2,3},{3,4},{4,5},{5,6},{6,7},{8,9},{9,10},{10,11},{11... | collective-permute-start | bytes 18440 | tf_op jit(solution)/shard_map/ppermute | solution.py:27
Sparse Core Ops, SparseCore 0:
  32.0 65.1 all-gather.1
where the time goes:
time: 160 us; the launch traced here: 159 us
  waiting for transfers between devices  87.3 us (55%)
  starting transfers between devices  38.3 us (24%)
  between operations  15.9 us (10%)
  other arithmetic  10.6 us (7%)
  local copies, waits for them, and re-layouts  7.37 us (5%)
    all_gather x1, waiting for transfers between devices, shards(): column_strip = lax.all_gather(ground_geometry, 'grp', axis=1, tiled=True)  55.6 us
    ppermute x6, waiting for transfers between devices, padded(): before = lax.ppermute(last, axis, up)  17.1 us
    ppermute x6, starting transfers between devices, padded(): after = lax.ppermute(leading, axis, down)  17.1 us
    ppermute x6, starting transfers between devices, padded(): before = lax.ppermute(last, axis, up)  15.2 us
    all_to_all x1, waiting for transfers between devices, shards(): lax.all_to_all(blocks, 'tile', split_axis=1, concat_axis=3, tiled=True)  11.5 us
    all_to_all x1, starting transfers between devices, shards(): lax.all_to_all(blocks, 'tile', split_axis=1, concat_axis=3, tiled=True)  6.03 us
  transfers between devices with their start and end apart: 14, of which 8 were waited for; matrix products, arithmetic and copies ran while one was open for 1% of the time, Pallas kernels for 0%

commit v1 on v0

v1 whole, which is shorter than its diff:
```python
import functools
import jax
import jax.numpy as jnp
from jax import lax
from jax.experimental import pallas as pl
from jax.experimental.pallas import tpu as pltpu
from jax.sharding import PartitionSpec as P

STEPS = 4
REACH = 3
LANES = 128
SUB = 8
PACKS = 16
CHUNK = 64

cell_size = 2.0
gravity = 9.81
time_step = 0.1
friction = 0.2
turbulence = 500.0
depth_floor = 0.1
speed_floor = 0.5
binomial = (0.0625, 0.25, 0.375, 0.25, 0.0625)
still_wave = (gravity * depth_floor) ** 0.5

MESH = pl.DeviceIdType.MESH


def shifted(x, by, axis):
    size = x.shape[axis]
    by = by % size
    return x if by == 0 else pltpu.roll(x, size - by, axis)


def five_taps(x, axis):
    outer = x + shifted(x, 4, axis)
    inner = shifted(x, 1, axis) + shifted(x, 3, axis)
    return binomial[0] * outer + binomial[1] * inner + binomial[2] * shifted(x, 2, axis)


def normal_fields(up, low, right, left, centre):
    grad_r = (up - low) * 0.25
    grad_c = (right - left) * 0.25
    curvature = (up + low + right + left - 4.0 * centre) * 0.25
    upright = lax.rsqrt(1.0 + grad_r * grad_r + grad_c * grad_c)
    return -grad_r * upright, -grad_c * upright, upright, curvature


def flow_step(state, patch, row_ok, col):
    depth, mom_r, mom_c = state
    n_r, n_c, n_z, kappa = patch
    width = depth.shape[1]
    inv = 1.0 / jnp.maximum(depth, depth_floor)
    u_r = mom_r * inv
    u_c = mom_c * inv
    wave = jnp.sqrt(gravity * (jnp.maximum(depth, 0.0) + depth_floor))
    pressure = 0.5 * gravity * depth * depth

    reach = jnp.abs(u_r) + wave
    bound = jnp.maximum(reach, shifted(reach, 1, 0))
    gains = []
    for q, f in (
        (depth, mom_r),
        (mom_r, mom_r * u_r + pressure),
        (mom_c, mom_c * u_r),
    ):
        face = (f + shifted(f, 1, 0)) - bound * (shifted(q, 1, 0) - q)
        gains.append(face - shifted(face, -1, 0))

    reach = jnp.abs(u_c) + wave
    last = col == width - 1
    first = col == 0
    bound = jnp.maximum(reach, jnp.where(last, still_wave, shifted(reach, 1, 1)))
    rim_bound = jnp.maximum(reach, still_wave)
    totals = []
    for gain, q, f in zip(
        gains,
        (depth, mom_r, mom_c),
        (mom_c, mom_r * u_c, mom_c * u_c + pressure),
    ):
        q_next = jnp.where(last, 0.0, shifted(q, 1, 1))
        f_next = jnp.where(last, 0.0, shifted(f, 1, 1))
        face = (f + f_next) - bound * (q_next - q)
        before = jnp.where(first, f - rim_bound * q, shifted(face, -1, 1))
        totals.append(gain + (face - before))

    scale = 0.5 * time_step / cell_size
    new_depth = depth - scale * totals[0]
    push = time_step * gravity * depth
    new_r = mom_r - scale * totals[1] + push * n_r
    new_c = mom_c - scale * totals[2] + push * n_c
    inv = 1.0 / jnp.maximum(new_depth, depth_floor)
    v_r = new_r * inv
    v_c = new_c * inv
    square = v_r * v_r + v_c * v_c
    energy = square + speed_floor * speed_floor
    inv_speed = lax.rsqrt(energy)
    load = jnp.maximum(gravity * n_z + kappa * square, 0.0)
    drag = time_step * (
        friction * load * inv_speed + (gravity / turbulence) * (energy * inv_speed) * inv
    )
    damp = 1.0 / (1.0 + drag)
    return (
        jnp.where(row_ok, new_depth, 0.0),
        jnp.where(row_ok, new_r * damp, 0.0),
        jnp.where(row_ok, new_c * damp, 0.0),
    )


def kernel(
    groups,
    tiles,
    north_ref,
    east_ref,
    trigger_ref,
    snow_ref,
    height_ref,
    geo_out,
    flow_out,
    high,
    side,
    smooth,
    diff_c,
    sum_c,
    geo,
    packed,
    packed_in,
    edge_in,
    depth_own,
    depth_in,
    index,
    strip_out,
    strip_in,
    strip,
    block_in,
    state,
    load_sem,
    store_sem,
    send_sem,
    recv_sem,
    strip_send,
    strip_recv,
    block_send,
    block_recv,
):
    g = lax.axis_index("grp")
    t = lax.axis_index("tile")
    rows = height_ref.shape[0]
    piece = trigger_ref.shape[1]
    width = trigger_ref.shape[2]
    span = strip.shape[0]
    block_rows = block_in.shape[1]
    window_rows = piece * tiles
    pad = span
    state_rows = piece + 2 * STEPS
    north_of = lambda d: lax.rem(g + d + groups, groups)
    east_of = lambda d: lax.rem(t + d + tiles, tiles)

    load = pltpu.make_async_copy(height_ref, high.at[pl.ds(pad, rows)], load_sem)
    load.start()

    barrier = pltpu.get_barrier_semaphore()
    peers = (
        [(north_of(d), t) for d in range(1, groups)]
        + [(g, east_of(d)) for d in range(1, tiles)]
        + [(north_of(a), east_of(b)) for a in (-1, 1) for b in (-1, 1)]
    )
    for peer in peers:
        pl.semaphore_signal(barrier, inc=1, device_id=peer, device_id_type=MESH)

    r0 = north_ref[0]
    c0 = east_ref[0]
    lane8 = lax.broadcasted_iota(jnp.int32, (SUB, LANES), 1)
    index[0] = jnp.zeros((SUB, LANES), jnp.int32) + r0
    zeros = jnp.zeros((pad, LANES), jnp.float32)
    high[pl.ds(0, pad), :] = zeros
    high[pl.ds(pad + rows, pad), :] = zeros
    own_depth = (
        trigger_ref[0].astype(jnp.float32) * snow_ref[0].astype(jnp.float32) * 0.01
    )
    depth_own[...] = own_depth

    pl.semaphore_wait(barrier, len(peers))

    def remote(src, dst, sends, recvs, slot, peer):
        return pltpu.make_async_remote_copy(
            src_ref=src,
            dst_ref=dst,
            send_sem=sends.at[slot],
            recv_sem=recvs.at[slot],
            device_id=peer,
            device_id_type=MESH,
        )

    index_copies = [
        remote(index.at[0], index.at[d], send_sem, recv_sem, d - 1, (north_of(d), t))
        for d in range(1, groups)
    ]
    for copy in index_copies:
        copy.start()

    load.wait()
    lower = high.at[pl.ds(pad, SUB)]
    upper = high.at[pl.ds(pad + rows - SUB, SUB)]
    halo_copies = []
    for b in (-1, 0, 1):
        halo_copies.append(
            remote(upper, edge_in.at[1 - b], send_sem, recv_sem, groups + 1 - b, (north_of(1), east_of(b)))
        )
        halo_copies.append(
            remote(lower, edge_in.at[4 - b], send_sem, recv_sem, groups + 4 - b, (north_of(-1), east_of(b)))
        )
    base = groups + 6
    halo_copies.append(
        remote(depth_own.at[pl.ds(piece - SUB, SUB)], depth_in.at[0], send_sem, recv_sem, base, (g, east_of(1)))
    )
    halo_copies.append(
        remote(depth_own.at[pl.ds(0, SUB)], depth_in.at[1], send_sem, recv_sem, base + 1, (g, east_of(-1)))
    )
    pack_rows = rows // PACKS
    lane_p = lax.broadcasted_iota(jnp.int32, (pack_rows, LANES), 1)
    step = LANES // PACKS

    strip_copies = []
    for d in range(groups):
        if d > 0:
            index_copies[d - 1].wait_recv()
            first = index[d][0, 0]
        else:
            first = r0
        scenario = north_of(-d)
        start = jnp.clip(first - (REACH + STEPS) - g * rows, -pad, rows) + pad
        part = high[pl.ds(start, span), :]
        if d > 0:
            strip_out[d] = part
            copy = remote(strip_out.at[d], strip_in.at[d], strip_send, strip_recv, d, (scenario, t))
            copy.start()
            strip_copies.append(copy)
        else:
            strip_in[0] = part

    total = jnp.zeros((pack_rows, LANES), jnp.float32)
    for k in range(PACKS):
        part = high[pl.ds(pad + k * pack_rows, pack_rows), :]
        both = jnp.where(lane_p < step // 2, part, pltpu.roll(part, step, 1))
        if k:
            both = pltpu.roll(both, step * k, 1)
        total = jnp.where(lane_p // step == k, both, total)
    packed[...] = total
    halo_copies.append(
        remote(packed, packed_in.at[0], send_sem, recv_sem, base + 2, (g, east_of(1)))
    )
    halo_copies.append(
        remote(packed, packed_in.at[1], send_sem, recv_sem, base + 3, (g, east_of(-1)))
    )
    for copy in halo_copies:
        copy.start()

    for copy in halo_copies:
        copy.wait()

    has_above = g > 0
    has_below = g < groups - 1
    has_left = t > 0
    has_right = t < tiles - 1
    right_half = lane8 < LANES // 2
    for at, slot, here in (
        (pad - SUB, 0, has_above),
        (pad + rows, 3, has_below),
    ):
        high[pl.ds(at, SUB), :] = jnp.where(here, edge_in[slot + 1], 0.0)
        right = jnp.where(jnp.logical_and(here, has_right), edge_in[slot + 2], 0.0)
        left = jnp.where(jnp.logical_and(here, has_left), edge_in[slot], 0.0)
        side[pl.ds(at - pad + 2 * SUB, SUB), :] = jnp.where(right_half, right, left)
    right = jnp.where(has_right, packed_in[1], 0.0)
    left = jnp.where(has_left, packed_in[0], 0.0)
    mixed = jnp.where(lane_p % step < step // 2, right, left)
    for k in range(PACKS):
        ahead = shifted(mixed, step * k, 1)
        behind = shifted(mixed, step * k + step, 1)
        side[pl.ds(2 * SUB + k * pack_rows, pack_rows), :] = jnp.where(
            lane_p < LANES // 2, ahead, behind
        )

    def smooth_rows(at, count):
        def down(ref, offset):
            o = at + offset
            return (
                binomial[0] * (ref[pl.ds(o - 2, count), :] + ref[pl.ds(o + 2, count), :])
                + binomial[1] * (ref[pl.ds(o - 1, count), :] + ref[pl.ds(o + 1, count), :])
                + binomial[2] * ref[pl.ds(o, count), :]
            )

        both = jnp.concatenate([down(high, pad - SUB), down(side, SUB)], axis=1)
        both = (
            binomial[0] * (shifted(both, -2, 1) + shifted(both, 2, 1))
            + binomial[1] * (shifted(both, -1, 1) + shifted(both, 1, 1))
            + binomial[2] * both
        )
        centre = both[:, :LANES]
        right = shifted(both, 1, 1)[:, :LANES]
        left = shifted(both, -1, 1)[:, :LANES]
        smooth[pl.ds(at, count), :] = centre
        diff_c[pl.ds(at, count), :] = right - left
        sum_c[pl.ds(at, count), :] = right + left - 4.0 * centre

    smooth_rows(0, SUB)
    smooth_rows(rows + SUB, SUB)

    def smooth_body(i, carry):
        smooth_rows(pl.multiple_of(SUB + i * CHUNK, SUB), CHUNK)
        return carry

    lax.fori_loop(0, rows // CHUNK, smooth_body, 0)

    for copy in strip_copies:
        copy.wait()
    row_at = lax.broadcasted_iota(jnp.int32, (span, LANES), 0) + (r0 - (REACH + STEPS))
    chosen = strip_in[0]
    for d in range(1, groups):
        source = north_of(d)
        inside = jnp.logical_and(row_at >= source * rows, row_at < source * rows + rows)
        chosen = jnp.where(inside, strip_in[d], chosen)
    strip[...] = chosen
    block_copies = []
    for d in range(1, tiles):
        to = east_of(d)
        copy = remote(
            strip.at[pl.ds(pl.multiple_of(to * piece, SUB), block_rows)],
            block_in.at[t],
            block_send,
            block_recv,
            d,
            (g, to),
        )
        copy.start()
        block_copies.append(copy)
    block_in[t] = strip[pl.ds(pl.multiple_of(t * piece, SUB), block_rows), :]

    def geo_body(i, carry):
        at = pl.multiple_of(i * CHUNK, SUB)
        up = smooth[pl.ds(at + SUB + 1, CHUNK), :]
        low = smooth[pl.ds(at + SUB - 1, CHUNK), :]
        grad_r = (up - low) * 0.25
        grad_c = diff_c[pl.ds(at + SUB, CHUNK), :] * 0.25
        upright = lax.rsqrt(1.0 + grad_r * grad_r + grad_c * grad_c)
        geo[0, pl.ds(at, CHUNK), :] = -grad_r * upright
        geo[1, pl.ds(at, CHUNK), :] = -grad_c * upright
        geo[2, pl.ds(at, CHUNK), :] = upright
        geo[3, pl.ds(at, CHUNK), :] = (up + low + sum_c[pl.ds(at + SUB, CHUNK), :]) * 0.25
        return carry

    lax.fori_loop(0, rows // CHUNK, geo_body, 0)
    store = pltpu.make_async_copy(geo, geo_out, store_sem)
    store.start()

    for copy in block_copies:
        copy.wait()

    first_col = c0 - REACH
    tile_at = lax.shift_right_logical(first_col, 7)
    lane_at = jnp.bitwise_and(first_col, LANES - 1)
    lane_b = lax.broadcasted_iota(jnp.int32, (block_rows, LANES), 1)
    turned = [
        pltpu.roll(block_in[jnp.minimum(tile_at + j, tiles - 1)], LANES - lane_at, 1)
        for j in range(width // LANES + 2)
    ]
    under = jnp.concatenate(
        [
            jnp.where(lane_b < LANES - lane_at, turned[j], turned[j + 1])
            for j in range(width // LANES + 1)
        ],
        axis=1,
    )
    level = five_taps(five_taps(under, 0), 1)
    middle = shifted(level, 1, 0)
    beside = shifted(level, 1, 1)
    patch = normal_fields(
        shifted(beside, 2, 0),
        beside,
        shifted(middle, 2, 1),
        middle,
        shifted(beside, 1, 0),
    )
    patch = tuple(field[:state_rows, :width] for field in patch)

    row = lax.broadcasted_iota(jnp.int32, (state_rows, width), 0) + (t * piece - STEPS)
    col = lax.broadcasted_iota(jnp.int32, (state_rows, width), 1)
    row_ok = jnp.logical_and(row >= 0, row < window_rows)
    depth = jnp.concatenate(
        [depth_in[0][SUB - STEPS :], depth_own[...], depth_in[1][:STEPS]], axis=0
    )
    depth = jnp.where(row_ok, depth, 0.0)
    state[0] = depth
    state[1] = jnp.zeros_like(depth)
    state[2] = jnp.zeros_like(depth)

    def flow_body(i, carry):
        new = flow_step((state[0], state[1], state[2]), patch, row_ok, col)
        for n in range(3):
            state[n] = new[n]
        return carry

    lax.fori_loop(0, STEPS, flow_body, 0)
    for n in range(3):
        flow_out[0, n] = state[n][STEPS : STEPS + piece]

    for copy in index_copies:
        copy.wait_send()
    store.wait()


def shards(height, trigger, snow, north, east):
    groups = lax.axis_size("grp")
    tiles = lax.axis_size("tile")
    rows, cols = height.shape
    _, piece, width = trigger.shape
    block_rows = -(-(piece + 2 * STEPS + 2 * REACH) // SUB) * SUB
    span = piece * (tiles - 1) + block_rows
    state_rows = piece + 2 * STEPS
    f32 = jnp.float32
    pack_rows = rows // PACKS
    vmem = pl.BlockSpec(memory_space=pltpu.VMEM)
    smem = pl.BlockSpec(memory_space=pltpu.SMEM)
    anywhere = pl.BlockSpec(memory_space=pl.ANY)
    dma = pltpu.SemaphoreType.DMA
    small = groups + 10
    return tuple(
        pl.pallas_call(
            functools.partial(kernel, groups, tiles),
            out_shape=(
                jax.ShapeDtypeStruct((4, rows, cols), f32),
                jax.ShapeDtypeStruct((1, 3, piece, width), f32),
            ),
            in_specs=[smem, smem, vmem, vmem, anywhere],
            out_specs=(anywhere, vmem),
            scratch_shapes=[
                pltpu.VMEM((rows + 2 * span, cols), f32),
                pltpu.VMEM((rows + 4 * SUB, LANES), f32),
                pltpu.VMEM((rows + 2 * SUB, LANES), f32),
                pltpu.VMEM((rows + 2 * SUB, LANES), f32),
                pltpu.VMEM((rows + 2 * SUB, LANES), f32),
                pltpu.VMEM((4, rows, cols), f32),
                pltpu.VMEM((pack_rows, LANES), f32),
                pltpu.VMEM((2, pack_rows, LANES), f32),
                pltpu.VMEM((6, SUB, LANES), f32),
                pltpu.VMEM((piece, width), f32),
                pltpu.VMEM((2, SUB, width), f32),
                pltpu.VMEM((groups, SUB, LANES), jnp.int32),
                pltpu.VMEM((groups, span, cols), f32),
                pltpu.VMEM((groups, span, cols), f32),
                pltpu.VMEM((span, cols), f32),
                pltpu.VMEM((tiles, block_rows, cols), f32),
                pltpu.VMEM((3, state_rows, width), f32),
                dma,
                dma,
                dma((small,)),
                dma((small,)),
                dma((groups,)),
                dma((groups,)),
                dma((tiles,)),
                dma((tiles,)),
            ],
            compiler_params=pltpu.CompilerParams(
                collective_id=0, has_side_effects=True, vmem_limit_bytes=48 * 1024 * 1024
            ),
        )(north, east, trigger, snow, height)
    )


def solution(mesh):
    return jax.shard_map(
        shards,
        mesh=mesh,
        in_specs=(
            P("grp", "tile"),
            P("grp", "tile", None),
            P("grp", "tile", None),
            P("grp"),
            P("grp"),
        ),
        out_specs=(P(None, "grp", "tile"), P("grp", None, "tile", None)),
        check_vma=False,
    )
```

time: 160 us -> 36.4 us (0.23)
  the two profiles are of different devices: /device:TPU:16 before, /device:TPU:0 now
where the time goes in v1:
time: 36.4 us; the launch traced here: 36.1 us
  Pallas kernels  29.4 us (81%)
  local copies, waits for them, and re-layouts  4.82 us (13%)
  between operations  1.94 us (5%)
    pallas_call x1, Pallas kernels, shards(): pl.pallas_call(functools.partial(kernel, groups, tiles), out_shape=(jax.S...  29.4 us
    unnamed x8, local copies, waits for them, and re-layouts  4.82 us

profile of v1, /device:TPU:0, one launch (start us, length us, event | category | flops | bytes accessed | tf_op | source)
XLA Modules:
  0.0 36.1 jit_solution(15166644651768353566)
XLA Ops:
  1.9 0.0 copy-start
  1.9 1.1 %copy-done = f32[1152,128]{1,0:T(8,128)S(1)} copy-done((f32[1152,128]{1,0:T(8,128)S(1)}, f32[1152,128]{1,0:T(8,128)}, u32[]{:S(2)}) %copy-start) | copy-done | bytes 589848
  3.0 0.0 copy-start.1
  3.0 0.8 %copy-done.1 = s32[1,32,512]{2,1,0:T(8,128)S(1)} copy-done((s32[1,32,512]{2,1,0:T(8,128)S(1)}, s32[1,32,512]{2,1,0:T(8,128)}, u32[]{:S(2)}) %copy-start.1) | copy-done | bytes 65560
  3.8 0.0 copy-start.2
  3.8 0.8 %copy-done.2 = s32[1,32,512]{2,1,0:T(8,128)S(1)} copy-done((s32[1,32,512]{2,1,0:T(8,128)S(1)}, s32[1,32,512]{2,1,0:T(8,128)}, u32[]{:S(2)}) %copy-start.2) | copy-done | bytes 65560
  4.7 29.4 %shard_map.68 = (f32[4,1152,128]{2,1,0:T(8,128)S(1)}, f32[1,3,32,512]{3,2,1,0:T(8,128)S(1)}) custom-call(s32[1]{0:T(128)S(6)} %copy.9.north_ref, s32[1]{0:T(128)S(6)} %copy.10.east_ref, s32[1,32,512]{2,1,0:T(8,128)S(1)} %copy-done.1, s32[1,32,512]{2,1,0:T(8,128)S(1)} %copy-done.2, f32[1152,128]{1,0:T(8,128)S(1)} %copy-done), custom_call_target="tpu_custom_call" | custom-call | tf_op jit(solution)/shard_map/pallas_call | solution.py:429
  34.0 1.4 %copy.11 = f32[4,1152,128]{2,1,0:T(8,128)} copy(f32[4,1152,128]{2,1,0:T(8,128)S(1)} %get-tuple-element.4) | data formatting | bytes 4718592
  35.4 0.7 %copy.12 = f32[1,3,32,512]{3,2,1,0:T(8,128)} copy(f32[1,3,32,512]{3,2,1,0:T(8,128)S(1)} %get-tuple-element.5) | data formatting | bytes 393216
Async XLA Ops:
  1.9 1.1 %copy-start = (f32[1152,128]{1,0:T(8,128)S(1)}, f32[1152,128]{1,0:T(8,128)}, u32[]{:S(2)}) copy-start(f32[1152,128]{1,0:T(8,128)} %height_ref.1) | copy-start | bytes 1769476
  3.0 0.8 %copy-start.1 = (s32[1,32,512]{2,1,0:T(8,128)S(1)}, s32[1,32,512]{2,1,0:T(8,128)}, u32[]{:S(2)}) copy-start(s32[1,32,512]{2,1,0:T(8,128)} %trigger_ref.1) | copy-start | bytes 196612
  3.8 0.8 %copy-start.2 = (s32[1,32,512]{2,1,0:T(8,128)S(1)}, s32[1,32,512]{2,1,0:T(8,128)}, u32[]{:S(2)}) copy-start(s32[1,32,512]{2,1,0:T(8,128)} %snow_ref.1) | copy-start | bytes 196612

commit v2 on v1

--- a/solution.py
+++ b/solution.py
@@ -12,6 +12,7 @@
 SUB = 8
 PACKS = 16
 CHUNK = 64
+VMEM_MIB = 60
 
 cell_size = 2.0
 gravity = 9.81
@@ -107,16 +108,16 @@
     )
 
 
-def kernel(
+def exchange(
     groups,
     tiles,
-    north_ref,
-    east_ref,
-    trigger_ref,
-    snow_ref,
-    height_ref,
+    north_hbm,
+    trigger_hbm,
+    snow_hbm,
+    height_hbm,
     geo_out,
-    flow_out,
+    block_out,
+    depth_out,
     high,
     side,
     smooth,
@@ -128,12 +129,14 @@
     edge_in,
     depth_own,
     depth_in,
+    depth_all,
     index,
     strip_out,
     strip_in,
     strip,
-    block_in,
-    state,
+    north_ref,
+    trigger_ref,
+    snow_ref,
     load_sem,
     store_sem,
     send_sem,
@@ -145,40 +148,69 @@
 ):
     g = lax.axis_index("grp")
     t = lax.axis_index("tile")
-    rows = height_ref.shape[0]
-    piece = trigger_ref.shape[1]
-    width = trigger_ref.shape[2]
+    rows = height_hbm.shape[0]
+    piece = trigger_hbm.shape[1]
+    width = trigger_hbm.shape[2]
     span = strip.shape[0]
-    block_rows = block_in.shape[1]
+    block_rows = block_out.shape[1]
     window_rows = piece * tiles
     pad = span
     state_rows = piece + 2 * STEPS
     north_of = lambda d: lax.rem(g + d + groups, groups)
     east_of = lambda d: lax.rem(t + d + tiles, tiles)
-
-    load = pltpu.make_async_copy(height_ref, high.at[pl.ds(pad, rows)], load_sem)
-    load.start()
+    other = g + 1 - 2 * lax.rem(g, 2)
+    across = lax.rem(g + 2, groups)
+    across_other = lax.rem(other + 2, groups)
+
+    loads = [
+        pltpu.make_async_copy(source, target, load_sem.at[n])
+        for n, (source, target) in enumerate(
+            (
+                (north_hbm, north_ref),
+                (height_hbm, high.at[pl.ds(pad, rows)]),
+                (trigger_hbm, trigger_ref),
+                (snow_hbm, snow_ref),
+            )
+        )
+    ]
+    for load in loads:
+        load.start()
 
     barrier = pltpu.get_barrier_semaphore()
     peers = (
-        [(north_of(d), t) for d in range(1, groups)]
+        [(other, t), (across, t), (across_other, t)]
         + [(g, east_of(d)) for d in range(1, tiles)]
         + [(north_of(a), east_of(b)) for a in (-1, 1) for b in (-1, 1)]
     )
     for peer in peers:
         pl.semaphore_signal(barrier, inc=1, device_id=peer, device_id_type=MESH)
 
+    lane8 = lax.broadcasted_iota(jnp.int32, (SUB, LANES), 1)
+    loads[0].wait()
     r0 = north_ref[0]
-    c0 = east_ref[0]
-    lane8 = lax.broadcasted_iota(jnp.int32, (SUB, LANES), 1)
     index[0] = jnp.zeros((SUB, LANES), jnp.int32) + r0
     zeros = jnp.zeros((pad, LANES), jnp.float32)
     high[pl.ds(0, pad), :] = zeros
     high[pl.ds(pad + rows, pad), :] = zeros
+    loads[2].wait()
+    loads[3].wait()
     own_depth = (
         trigger_ref[0].astype(jnp.float32) * snow_ref[0].astype(jnp.float32) * 0.01
     )
     depth_own[...] = own_depth
+
+    loads[1].wait()
+    pack_rows = rows // PACKS
+    lane_p = lax.broadcasted_iota(jnp.int32, (pack_rows, LANES), 1)
+    step = LANES // PACKS
+    total = jnp.zeros((pack_rows, LANES), jnp.float32)
+    for k in range(PACKS):
+        part = high[pl.ds(pad + k * pack_rows, pack_rows), :]
+        both = jnp.where(lane_p < step // 2, part, pltpu.roll(part, step, 1))
+        if k:
+            both = pltpu.roll(both, step * k, 1)
+        total = jnp.where(lane_p // step == k, both, total)
+    packed[...] = total
 
     pl.semaphore_wait(barrier, len(peers))
 
@@ -193,16 +225,16 @@
         )
 
     index_copies = [
-        remote(index.at[0], index.at[d], send_sem, recv_sem, d - 1, (north_of(d), t))
-        for d in range(1, groups)
-    ]
-    for copy in index_copies:
-        copy.start()
-
-    load.wait()
+        remote(index.at[0], index.at[d], send_sem, recv_sem, d - 1, (peer, t))
+        for d, peer in ((3, across_other), (2, across), (1, other))
+    ]
     lower = high.at[pl.ds(pad, SUB)]
     upper = high.at[pl.ds(pad + rows - SUB, SUB)]
-    halo_copies = []
+    base = groups + 6
+    halo_copies = [
+        remote(packed, packed_in.at[0], send_sem, recv_sem, base + 2, (g, east_of(1))),
+        remote(packed, packed_in.at[1], send_sem, recv_sem, base + 3, (g, east_of(-1))),
+    ]
     for b in (-1, 0, 1):
         halo_copies.append(
             remote(upper, edge_in.at[1 - b], send_sem, recv_sem, groups + 1 - b, (north_of(1), east_of(b)))
@@ -210,51 +242,39 @@
         halo_copies.append(
             remote(lower, edge_in.at[4 - b], send_sem, recv_sem, groups + 4 - b, (north_of(-1), east_of(b)))
         )
-    base = groups + 6
-    halo_copies.append(
-        remote(depth_own.at[pl.ds(piece - SUB, SUB)], depth_in.at[0], send_sem, recv_sem, base, (g, east_of(1)))
-    )
-    halo_copies.append(
-        remote(depth_own.at[pl.ds(0, SUB)], depth_in.at[1], send_sem, recv_sem, base + 1, (g, east_of(-1)))
-    )
-    pack_rows = rows // PACKS
-    lane_p = lax.broadcasted_iota(jnp.int32, (pack_rows, LANES), 1)
-    step = LANES // PACKS
-
-    strip_copies = []
-    for d in range(groups):
-        if d > 0:
-            index_copies[d - 1].wait_recv()
-            first = index[d][0, 0]
-        else:
-            first = r0
-        scenario = north_of(-d)
+    depth_copies = [
+        remote(depth_own.at[pl.ds(piece - SUB, SUB)], depth_in.at[0], send_sem, recv_sem, base, (g, east_of(1))),
+        remote(depth_own.at[pl.ds(0, SUB)], depth_in.at[1], send_sem, recv_sem, base + 1, (g, east_of(-1))),
+    ]
+    for copy in index_copies + halo_copies + depth_copies:
+        copy.start()
+
+    def part_of(first):
         start = jnp.clip(first - (REACH + STEPS) - g * rows, -pad, rows) + pad
-        part = high[pl.ds(start, span), :]
-        if d > 0:
-            strip_out[d] = part
-            copy = remote(strip_out.at[d], strip_in.at[d], strip_send, strip_recv, d, (scenario, t))
-            copy.start()
-            strip_copies.append(copy)
-        else:
-            strip_in[0] = part
-
-    total = jnp.zeros((pack_rows, LANES), jnp.float32)
-    for k in range(PACKS):
-        part = high[pl.ds(pad + k * pack_rows, pack_rows), :]
-        both = jnp.where(lane_p < step // 2, part, pltpu.roll(part, step, 1))
-        if k:
-            both = pltpu.roll(both, step * k, 1)
-        total = jnp.where(lane_p // step == k, both, total)
-    packed[...] = total
-    halo_copies.append(
-        remote(packed, packed_in.at[0], send_sem, recv_sem, base + 2, (g, east_of(1)))
-    )
-    halo_copies.append(
-        remote(packed, packed_in.at[1], send_sem, recv_sem, base + 3, (g, east_of(-1)))
-    )
-    for copy in halo_copies:
-        copy.start()
+        return high[pl.ds(start, span), :]
+
+    index_copies[0].wait_recv()
+    strip_out[0] = part_of(index[3][0, 0])
+    far = remote(strip_out.at[0], strip_in.at[0], strip_send, strip_recv, 0, (other, t))
+    far.start()
+    index_copies[2].wait_recv()
+    strip_out[1] = part_of(index[1][0, 0])
+    near = remote(strip_out.at[1], strip_in.at[1], strip_send, strip_recv, 1, (other, t))
+    near.start()
+    index_copies[1].wait_recv()
+    first_across = index[2][0, 0]
+    strip_out[2] = part_of(first_across)
+    strip[...] = part_of(r0)
+
+    row_in = lax.broadcasted_iota(jnp.int32, (span, LANES), 0) - (REACH + STEPS)
+
+    def of_block(first, block):
+        return jnp.logical_and(row_in >= block * rows - first, row_in < (block + 1) * rows - first)
+
+    far.wait()
+    strip_out[2] = jnp.where(of_block(first_across, other), strip_in[0], strip_out[2])
+    long = remote(strip_out.at[2], strip_in.at[2], strip_send, strip_recv, 2, (across, t))
+    long.start()
 
     for copy in halo_copies:
         copy.wait()
@@ -272,6 +292,8 @@
         right = jnp.where(jnp.logical_and(here, has_right), edge_in[slot + 2], 0.0)
         left = jnp.where(jnp.logical_and(here, has_left), edge_in[slot], 0.0)
         side[pl.ds(at - pad + 2 * SUB, SUB), :] = jnp.where(right_half, right, left)
+    side[pl.ds(0, SUB), :] = jnp.zeros((SUB, LANES), jnp.float32)
+    side[pl.ds(rows + 3 * SUB, SUB), :] = jnp.zeros((SUB, LANES), jnp.float32)
     right = jnp.where(has_right, packed_in[1], 0.0)
     left = jnp.where(has_left, packed_in[0], 0.0)
     mixed = jnp.where(lane_p % step < step // 2, right, left)
@@ -313,21 +335,19 @@
 
     lax.fori_loop(0, rows // CHUNK, smooth_body, 0)
 
-    for copy in strip_copies:
-        copy.wait()
-    row_at = lax.broadcasted_iota(jnp.int32, (span, LANES), 0) + (r0 - (REACH + STEPS))
-    chosen = strip_in[0]
-    for d in range(1, groups):
-        source = north_of(d)
-        inside = jnp.logical_and(row_at >= source * rows, row_at < source * rows + rows)
-        chosen = jnp.where(inside, strip_in[d], chosen)
-    strip[...] = chosen
+    near.wait()
+    long.wait()
+    strip[...] = jnp.where(
+        of_block(r0, g),
+        strip[...],
+        jnp.where(of_block(r0, other), strip_in[1], strip_in[2]),
+    )
     block_copies = []
     for d in range(1, tiles):
         to = east_of(d)
         copy = remote(
             strip.at[pl.ds(pl.multiple_of(to * piece, SUB), block_rows)],
-            block_in.at[t],
+            block_out.at[t],
             block_send,
             block_recv,
             d,
@@ -335,7 +355,25 @@
         )
         copy.start()
         block_copies.append(copy)
-    block_in[t] = strip[pl.ds(pl.multiple_of(t * piece, SUB), block_rows), :]
+    stores = [
+        pltpu.make_async_copy(
+            strip.at[pl.ds(pl.multiple_of(t * piece, SUB), block_rows)],
+            block_out.at[t],
+            store_sem.at[0],
+        )
+    ]
+    stores[0].start()
+
+    for copy in depth_copies:
+        copy.wait()
+    row = lax.broadcasted_iota(jnp.int32, (state_rows, width), 0) + (t * piece - STEPS)
+    row_ok = jnp.logical_and(row >= 0, row < window_rows)
+    depth = jnp.concatenate(
+        [depth_in[0][SUB - STEPS :], depth_own[...], depth_in[1][:STEPS]], axis=0
+    )
+    depth_all[...] = jnp.where(row_ok, depth, 0.0)
+    stores.append(pltpu.make_async_copy(depth_all, depth_out, store_sem.at[1]))
+    stores[1].start()
 
     def geo_body(i, carry):
         at = pl.multiple_of(i * CHUNK, SUB)
@@ -351,13 +389,55 @@
         return carry
 
     lax.fori_loop(0, rows // CHUNK, geo_body, 0)
-    store = pltpu.make_async_copy(geo, geo_out, store_sem)
-    store.start()
+    stores.append(pltpu.make_async_copy(geo, geo_out, store_sem.at[2]))
+    stores[2].start()
 
     for copy in block_copies:
         copy.wait()
-
-    first_col = c0 - REACH
+    for copy in index_copies:
+        copy.wait_send()
+    for store in stores:
+        store.wait()
+
+
+def flow(
+    tiles,
+    east_hbm,
+    geo_in,
+    block_hbm,
+    depth_hbm,
+    geo_out,
+    flow_out,
+    east_ref,
+    block_in,
+    state,
+    result,
+    geo_held,
+    load_sem,
+    geo_sem,
+    store_sem,
+):
+    t = lax.axis_index("tile")
+    state_rows, width = depth_hbm.shape
+    piece = state_rows - 2 * STEPS
+    block_rows = block_in.shape[1]
+    loads = [
+        pltpu.make_async_copy(source, target, load_sem.at[n])
+        for n, (source, target) in enumerate(
+            ((east_hbm, east_ref), (block_hbm, block_in), (depth_hbm, state.at[0]))
+        )
+    ]
+    for load in loads:
+        load.start()
+    geo_loads = [
+        pltpu.make_async_copy(geo_in.at[n], geo_held.at[n], geo_sem.at[n]) for n in range(4)
+    ]
+    for load in geo_loads:
+        load.start()
+    for load in loads:
+        load.wait()
+
+    first_col = east_ref[0] - REACH
     tile_at = lax.shift_right_logical(first_col, 7)
     lane_at = jnp.bitwise_and(first_col, LANES - 1)
     lane_b = lax.broadcasted_iota(jnp.int32, (block_rows, LANES), 1)
@@ -383,17 +463,17 @@
         shifted(beside, 1, 0),
     )
     patch = tuple(field[:state_rows, :width] for field in patch)
+    geo_stores = []
+    for n in range(4):
+        geo_loads[n].wait()
+        geo_stores.append(pltpu.make_async_copy(geo_held.at[n], geo_out.at[n], geo_sem.at[4 + n]))
+        geo_stores[n].start()
 
     row = lax.broadcasted_iota(jnp.int32, (state_rows, width), 0) + (t * piece - STEPS)
     col = lax.broadcasted_iota(jnp.int32, (state_rows, width), 1)
-    row_ok = jnp.logical_and(row >= 0, row < window_rows)
-    depth = jnp.concatenate(
-        [depth_in[0][SUB - STEPS :], depth_own[...], depth_in[1][:STEPS]], axis=0
-    )
-    depth = jnp.where(row_ok, depth, 0.0)
-    state[0] = depth
-    state[1] = jnp.zeros_like(depth)
-    state[2] = jnp.zeros_like(depth)
+    row_ok = jnp.logical_and(row >= 0, row < piece * tiles)
+    state[1] = jnp.zeros((state_rows, width), jnp.float32)
+    state[2] = jnp.zeros((state_rows, width), jnp.float32)
 
     def flow_body(i, carry):
         new = flow_step((state[0], state[1], state[2]), patch, row_ok, col)
@@ -403,11 +483,12 @@
 
     lax.fori_loop(0, STEPS, flow_body, 0)
     for n in range(3):
-        flow_out[0, n] = state[n][STEPS : STEPS + piece]
-
-    for copy in index_copies:
-        copy.wait_send()
+        result[0, n] = state[n][STEPS : STEPS + piece]
+    store = pltpu.make_async_copy(result, flow_out, store_sem)
+    store.start()
     store.wait()
+    for copy in geo_stores:
+        copy.wait()
 
 
 def shards(height, trigger, snow, north, east):
@@ -415,56 +496,79 @@
     tiles = lax.axis_size("tile")
     rows, cols = height.shape
     _, piece, width = trigger.shape
+    assert groups == 4 and cols == LANES and rows % (PACKS * SUB) == 0 and rows % CHUNK == 0
     block_rows = -(-(piece + 2 * STEPS + 2 * REACH) // SUB) * SUB
     span = piece * (tiles - 1) + block_rows
     state_rows = piece + 2 * STEPS
     f32 = jnp.float32
     pack_rows = rows // PACKS
-    vmem = pl.BlockSpec(memory_space=pltpu.VMEM)
-    smem = pl.BlockSpec(memory_space=pltpu.SMEM)
     anywhere = pl.BlockSpec(memory_space=pl.ANY)
     dma = pltpu.SemaphoreType.DMA
     small = groups + 10
+    mib = 1024 * 1024
+    geo, blocks, depth = pl.pallas_call(
+        functools.partial(exchange, groups, tiles),
+        out_shape=(
+            jax.ShapeDtypeStruct((4, rows, cols), f32),
+            jax.ShapeDtypeStruct((tiles, block_rows, cols), f32),
+            jax.ShapeDtypeStruct((state_rows, width), f32),
+        ),
+        in_specs=[anywhere] * 4,
+        out_specs=(anywhere,) * 3,
+        scratch_shapes=[
+            pltpu.VMEM((rows + 2 * span, cols), f32),
+            pltpu.VMEM((rows + 4 * SUB, LANES), f32),
+            pltpu.VMEM((rows + 2 * SUB, LANES), f32),
+            pltpu.VMEM((rows + 2 * SUB, LANES), f32),
+            pltpu.VMEM((rows + 2 * SUB, LANES), f32),
+            pltpu.VMEM((4, rows, cols), f32),
+            pltpu.VMEM((pack_rows, LANES), f32),
+            pltpu.VMEM((2, pack_rows, LANES), f32),
+            pltpu.VMEM((6, SUB, LANES), f32),
+            pltpu.VMEM((piece, width), f32),
+            pltpu.VMEM((2, SUB, width), f32),
+            pltpu.VMEM((state_rows, width), f32),
+            pltpu.VMEM((groups, SUB, LANES), jnp.int32),
+            pltpu.VMEM((3, span, cols), f32),
+            pltpu.VMEM((3, span, cols), f32),
+            pltpu.VMEM((span, cols), f32),
+            pltpu.SMEM((1,), jnp.int32),
+            pltpu.VMEM((1, piece, width), jnp.int32),
+            pltpu.VMEM((1, piece, width), jnp.int32),
+            dma((4,)),
+            dma((3,)),
+            dma((small,)),
+            dma((small,)),
+            dma((3,)),
+            dma((3,)),
+            dma((tiles,)),
+            dma((tiles,)),
+        ],
+        compiler_params=pltpu.CompilerParams(
+            collective_id=0, has_side_effects=True, vmem_limit_bytes=VMEM_MIB * mib
+        ),
+    )(north, trigger, snow, height)
     return tuple(
         pl.pallas_call(
-            functools.partial(kernel, groups, tiles),
+            functools.partial(flow, tiles),
             out_shape=(
                 jax.ShapeDtypeStruct((4, rows, cols), f32),
                 jax.ShapeDtypeStruct((1, 3, piece, width), f32),
             ),
-            in_specs=[smem, smem, vmem, vmem, anywhere],
-            out_specs=(anywhere, vmem),
+            in_specs=[anywhere] * 4,
+            out_specs=(anywhere,) * 2,
             scratch_shapes=[
-                pltpu.VMEM((rows + 2 * span, cols), f32),
-                pltpu.VMEM((rows + 4 * SUB, LANES), f32),
-                pltpu.VMEM((rows + 2 * SUB, LANES), f32),
-                pltpu.VMEM((rows + 2 * SUB, LANES), f32),
-                pltpu.VMEM((rows + 2 * SUB, LANES), f32),
-                pltpu.VMEM((4, rows, cols), f32),
-                pltpu.VMEM((pack_rows, LANES), f32),
-                pltpu.VMEM((2, pack_rows, LANES), f32),
-                pltpu.VMEM((6, SUB, LANES), f32),
-                pltpu.VMEM((piece, width), f32),
-                pltpu.VMEM((2, SUB, width), f32),
-                pltpu.VMEM((groups, SUB, LANES), jnp.int32),
-                pltpu.VMEM((groups, span, cols), f32),
-                pltpu.VMEM((groups, span, cols), f32),
-                pltpu.VMEM((span, cols), f32),
+                pltpu.SMEM((1,), jnp.int32),
                 pltpu.VMEM((tiles, block_rows, cols), f32),
                 pltpu.VMEM((3, state_rows, width), f32),
+                pltpu.VMEM((1, 3, piece, width), f32),
+                pltpu.VMEM((4, rows, cols), f32),
+                dma((3,)),
+                dma((8,)),
                 dma,
-                dma,
-                dma((small,)),
-                dma((small,)),
-                dma((groups,)),
-                dma((groups,)),
-                dma((tiles,)),
-                dma((tiles,)),
             ],
-            compiler_params=pltpu.CompilerParams(
-                collective_id=0, has_side_effects=True, vmem_limit_bytes=48 * 1024 * 1024
-            ),
-        )(north, east, trigger, snow, height)
+            compiler_params=pltpu.CompilerParams(vmem_limit_bytes=VMEM_MIB * mib),
+        )(east, geo, blocks, depth)
     )
 
 

time: 36.4 us -> 28.1 us (0.77)
  local copies, waits for them, and re-layouts: 4.82 us -> 0 us
  Pallas kernels: 29.4 us -> 25.9 us
    unnamed x8 -> x0, local copies, waits for them, and re-layouts: 4.82 us -> none
    pallas_call x1 -> x2, Pallas kernels: 29.4 us -> 25.9 us  [the longest x1 21.1 us: shards(): pl.pallas_call(functools.partial(exchange, groups, tiles), out_shape=(jax...]
where the time goes in v2:
time: 28.1 us; the launch traced here: 27.9 us
  Pallas kernels  25.9 us (92%)
  between operations  1.93 us (7%)
    pallas_call x1, Pallas kernels, shards(): pl.pallas_call(functools.partial(exchange, groups, tiles), out_shape=(jax...  21.1 us
    pallas_call x1, Pallas kernels, shards(): pl.pallas_call(functools.partial(flow, tiles), out_shape=(jax.ShapeDtypeS...  4.89 us

profile of v2, /device:TPU:0, one launch (start us, length us, event | category | flops | bytes accessed | tf_op | source)
XLA Modules:
  0.0 27.9 jit_solution(13351144176952081437)
XLA Ops:
  1.9 21.1 %shard_map.68 = (f32[4,1152,128]{2,1,0:T(8,128)}, f32[8,48,128]{2,1,0:T(8,128)}, f32[40,512]{1,0:T(8,128)}) custom-call(s32[1]{0:T(128)S(6)} %copy.7.north_hbm, s32[1,32,512]{2,1,0:T(8,128)} %trigger_hbm.1, s32[1,32,512]{2,1,0:T(8,128)} %snow_hbm.1, f32[1152,128]{1,0:T(8,128)} %height_hbm.1), custom_call_target="tpu_custom_call" | custom-call | tf_op jit(solution)/shard_map/pallas_call | solution.py:509
  23.0 4.9 %shard_map.69 = (f32[4,1152,128]{2,1,0:T(8,128)}, f32[1,3,32,512]{3,2,1,0:T(8,128)}) custom-call(s32[1]{0:T(128)S(6)} %copy.8.east_hbm, f32[4,1152,128]{2,1,0:T(8,128)} %get-tuple-element.5.geo_in, f32[8,48,128]{2,1,0:T(8,128)} %get-tuple-element.6.block_hbm, f32[40,512]{1,0:T(8,128)} %get-tuple-element.7.depth_hbm), custom_call_target="tpu_custom_call" | custom-call | tf_op jit(solution)/shard_map/pallas_call | solution.py:552

commit v3 on v2

--- a/solution.py
+++ b/solution.py
@@ -49,7 +49,6 @@
 
 def flow_step(state, patch, row_ok, col):
     depth, mom_r, mom_c = state
-    n_r, n_c, n_z, kappa = patch
     width = depth.shape[1]
     inv = 1.0 / jnp.maximum(depth, depth_floor)
     u_r = mom_r * inv
@@ -85,6 +84,11 @@
         before = jnp.where(first, f - rim_bound * q, shifted(face, -1, 1))
         totals.append(gain + (face - before))
 
+    return finish_step(depth, mom_r, mom_c, totals, patch, row_ok)
+
+
+def finish_step(depth, mom_r, mom_c, totals, patch, row_ok):
+    n_r, n_c, n_z, kappa = patch
     scale = 0.5 * time_step / cell_size
     new_depth = depth - scale * totals[0]
     push = time_step * gravity * depth
@@ -106,6 +110,28 @@
         jnp.where(row_ok, new_r * damp, 0.0),
         jnp.where(row_ok, new_c * damp, 0.0),
     )
+
+
+def first_flow_step(depth, patch, row_ok, col):
+    width = depth.shape[1]
+    wave = jnp.sqrt(gravity * (jnp.maximum(depth, 0.0) + depth_floor))
+    pressure = 0.5 * gravity * depth * depth
+
+    bound = jnp.maximum(wave, shifted(wave, 1, 0))
+    face = bound * (depth - shifted(depth, 1, 0))
+    gain = face - shifted(face, -1, 0)
+    gain_r = shifted(pressure, 1, 0) - shifted(pressure, -1, 0)
+
+    last = col == width - 1
+    first = col == 0
+    bound = jnp.maximum(wave, jnp.where(last, still_wave, shifted(wave, 1, 1)))
+    face = bound * (depth - jnp.where(last, 0.0, shifted(depth, 1, 1)))
+    before = jnp.where(first, -jnp.maximum(wave, still_wave) * depth, shifted(face, -1, 1))
+    gain = gain + (face - before)
+    gain_c = jnp.where(last, 0.0, shifted(pressure, 1, 1)) - jnp.where(
+        first, 0.0, shifted(pressure, -1, 1)
+    )
+    return finish_step(depth, 0.0, 0.0, (gain, gain_r, gain_c), patch, row_ok)
 
 
 def exchange(
@@ -472,8 +498,9 @@
     row = lax.broadcasted_iota(jnp.int32, (state_rows, width), 0) + (t * piece - STEPS)
     col = lax.broadcasted_iota(jnp.int32, (state_rows, width), 1)
     row_ok = jnp.logical_and(row >= 0, row < piece * tiles)
-    state[1] = jnp.zeros((state_rows, width), jnp.float32)
-    state[2] = jnp.zeros((state_rows, width), jnp.float32)
+    new = first_flow_step(state[0], patch, row_ok, col)
+    for n in range(3):
+        state[n] = new[n]
 
     def flow_body(i, carry):
         new = flow_step((state[0], state[1], state[2]), patch, row_ok, col)
@@ -481,7 +508,7 @@
             state[n] = new[n]
         return carry
 
-    lax.fori_loop(0, STEPS, flow_body, 0)
+    lax.fori_loop(1, STEPS, flow_body, 0)
     for n in range(3):
         result[0, n] = state[n][STEPS : STEPS + piece]
     store = pltpu.make_async_copy(result, flow_out, store_sem)

time: 28.1 us -> 27.8 us (0.989)
  no operation moved by 1% of the time
where the time goes in v3:
time: 27.8 us; the launch traced here: 27.6 us
  Pallas kernels  25.7 us (92%)
  between operations  1.93 us (7%)
    pallas_call x1, Pallas kernels, shards(): pl.pallas_call(functools.partial(exchange, groups, tiles), out_shape=(jax...  21.1 us
    pallas_call x1, Pallas kernels, shards(): pl.pallas_call(functools.partial(flow, tiles), out_shape=(jax.ShapeDtypeS...  4.64 us

profile of v3, /device:TPU:0, one launch (start us, length us, event | category | flops | bytes accessed | tf_op | source)
XLA Modules:
  0.0 27.6 jit_solution(1500031826868267360)
XLA Ops:
  1.9 21.1 %shard_map.68 = (f32[4,1152,128]{2,1,0:T(8,128)}, f32[8,48,128]{2,1,0:T(8,128)}, f32[40,512]{1,0:T(8,128)}) custom-call(s32[1]{0:T(128)S(6)} %copy.7.north_hbm, s32[1,32,512]{2,1,0:T(8,128)} %trigger_hbm.1, s32[1,32,512]{2,1,0:T(8,128)} %snow_hbm.1, f32[1152,128]{1,0:T(8,128)} %height_hbm.1), custom_call_target="tpu_custom_call" | custom-call | tf_op jit(solution)/shard_map/pallas_call | solution.py:536
  23.0 4.6 %shard_map.69 = (f32[4,1152,128]{2,1,0:T(8,128)}, f32[1,3,32,512]{3,2,1,0:T(8,128)}) custom-call(s32[1]{0:T(128)S(6)} %copy.8.east_hbm, f32[4,1152,128]{2,1,0:T(8,128)} %get-tuple-element.5.geo_in, f32[8,48,128]{2,1,0:T(8,128)} %get-tuple-element.6.block_hbm, f32[40,512]{1,0:T(8,128)} %get-tuple-element.7.depth_hbm), custom_call_target="tpu_custom_call" | custom-call | tf_op jit(solution)/shard_map/pallas_call | solution.py:579

commit v4 on v3

--- a/solution.py
+++ b/solution.py
@@ -283,24 +283,24 @@
     strip_out[0] = part_of(index[3][0, 0])
     far = remote(strip_out.at[0], strip_in.at[0], strip_send, strip_recv, 0, (other, t))
     far.start()
+    index_copies[1].wait_recv()
+    first_across = index[2][0, 0]
+    strip_out[2] = part_of(first_across)
+
+    row_in = lax.broadcasted_iota(jnp.int32, (span, LANES), 0) - (REACH + STEPS)
+
+    def of_block(first, block):
+        return jnp.logical_and(row_in >= block * rows - first, row_in < (block + 1) * rows - first)
+
+    far.wait()
+    strip_out[2] = jnp.where(of_block(first_across, other), strip_in[0], strip_out[2])
+    long = remote(strip_out.at[2], strip_in.at[2], strip_send, strip_recv, 2, (across, t))
+    long.start()
     index_copies[2].wait_recv()
     strip_out[1] = part_of(index[1][0, 0])
     near = remote(strip_out.at[1], strip_in.at[1], strip_send, strip_recv, 1, (other, t))
     near.start()
-    index_copies[1].wait_recv()
-    first_across = index[2][0, 0]
-    strip_out[2] = part_of(first_across)
     strip[...] = part_of(r0)
-
-    row_in = lax.broadcasted_iota(jnp.int32, (span, LANES), 0) - (REACH + STEPS)
-
-    def of_block(first, block):
-        return jnp.logical_and(row_in >= block * rows - first, row_in < (block + 1) * rows - first)
-
-    far.wait()
-    strip_out[2] = jnp.where(of_block(first_across, other), strip_in[0], strip_out[2])
-    long = remote(strip_out.at[2], strip_in.at[2], strip_send, strip_recv, 2, (across, t))
-    long.start()
 
     for copy in halo_copies:
         copy.wait()

time: 27.8 us -> 27.8 us (level)
  no operation moved by 1% of the time
where the time goes in v4:
time: 27.8 us; the launch traced here: 27.6 us
  Pallas kernels  25.7 us (92%)
  between operations  1.93 us (7%)
    pallas_call x1, Pallas kernels, shards(): pl.pallas_call(functools.partial(exchange, groups, tiles), out_shape=(jax...  21.1 us
    pallas_call x1, Pallas kernels, shards(): pl.pallas_call(functools.partial(flow, tiles), out_shape=(jax.ShapeDtypeS...  4.64 us

profile of v4, /device:TPU:0, one launch (start us, length us, event | category | flops | bytes accessed | tf_op | source)
XLA Modules:
  0.0 27.6 jit_solution(6294940927462029315)
XLA Ops:
  1.9 21.1 %shard_map.68 = (f32[4,1152,128]{2,1,0:T(8,128)}, f32[8,48,128]{2,1,0:T(8,128)}, f32[40,512]{1,0:T(8,128)}) custom-call(s32[1]{0:T(128)S(6)} %copy.7.north_hbm, s32[1,32,512]{2,1,0:T(8,128)} %trigger_hbm.1, s32[1,32,512]{2,1,0:T(8,128)} %snow_hbm.1, f32[1152,128]{1,0:T(8,128)} %height_hbm.1), custom_call_target="tpu_custom_call" | custom-call | tf_op jit(solution)/shard_map/pallas_call | solution.py:536
  23.0 4.6 %shard_map.69 = (f32[4,1152,128]{2,1,0:T(8,128)}, f32[1,3,32,512]{3,2,1,0:T(8,128)}) custom-call(s32[1]{0:T(128)S(6)} %copy.8.east_hbm, f32[4,1152,128]{2,1,0:T(8,128)} %get-tuple-element.5.geo_in, f32[8,48,128]{2,1,0:T(8,128)} %get-tuple-element.6.block_hbm, f32[40,512]{1,0:T(8,128)} %get-tuple-element.7.depth_hbm), custom_call_target="tpu_custom_call" | custom-call | tf_op jit(solution)/shard_map/pallas_call | solution.py:579
